TPU v7x, 256 devices: a whole 4x4x8 slice. The times are simulated.
256 devices in a mesh: gx: 4 (over z_hi), gy: 64 (over y, z_lo, x, core).
Axes of the slice: x: 4, y: 4, z: 8 (z_hi: 4, z_lo: 2; z = z_hi * 2 + z_lo), core: 2. Of those that a mesh axis runs over, the one named last changes fastest.
Arguments:
- tokens: bfloat16 [1024, 16384], P(None, ('gx', 'gy')), may hold values from -6 to 6
- gate_weight: bfloat16 [16384, 32768], P('gx', 'gy'), may hold values from -0.046875 to 0.046875
- up_weight: bfloat16 [16384, 32768], P('gx', 'gy'), may hold values from -0.046875 to 0.046875
- down_weight: bfloat16 [32768, 16384], P('gy', 'gx'), may hold values from -0.03125 to 0.03125
Outputs:
- mixed: bfloat16 [1024, 16384], P('gy', 'gx')
All inputs are finite; a program needn't handle non-finite values.
Results may differ from a plain program's by a relative error of at most 0.0049.
Values may be sent and summed in bfloat16 or wider, within the bound.
A program may use at most 128 MiB of HBM per device.

v0:
```python
import jax
import jax.numpy as jnp
from jax import lax
from jax.sharding import PartitionSpec as P


def local(tokens, gate_weight, up_weight, down_weight):
    piece = lax.all_gather(tokens, "gy", axis=1, tiled=True)
    gate_next = jnp.dot(piece, gate_weight, preferred_element_type=jnp.float32)
    up_next = jnp.dot(piece, up_weight, preferred_element_type=jnp.float32)
    gate, up = lax.psum((gate_next, up_next), "gx")
    hidden = (jax.nn.silu(gate) * up).astype(jnp.bfloat16)
    terms = jnp.dot(hidden, down_weight, preferred_element_type=jnp.float32)
    mixed = lax.psum_scatter(terms, "gy", scatter_dimension=0, tiled=True)
    return mixed.astype(jnp.bfloat16)


def solution(mesh):
    placed = (P(None, ("gx", "gy")), P("gx", "gy"), P("gx", "gy"), P("gy", "gx"))
    return jax.shard_map(
        local, mesh=mesh, in_specs=placed, out_specs=P("gy", "gx"), check_vma=False
    )
```

profile of v0, /device:TPU:1, one launch (start us, length us, event | category | flops | bytes accessed | tf_op | source)
XLA Modules:
  0.0 639.1 jit_solution(14541143460897888325)
XLA Ops:
  6.5 0.0 all-gather.2.cloned.1.call-start
  6.5 0.7 all-gather.2.cloned.1.call-update
  7.3 0.0 all-reduce.3.cloned.1.call-start
  7.3 119.8 %all-gather.2.cloned.1.call-done = bf16[1024,4096]{0,1:T(8,128)(2,1)} async-done(((bf16[1024,64]{0,1:T(8,128)(2,1)}), bf16[1024,4096]{0,1:T(8,128)(2,1)}) %all-gather.2.cloned.1.call-update) | async-done | bytes 8388624 | tf_op jit(solution)/shard_map/all_gather | solution.py:8
  127.1 0.0 copy-start
  127.1 0.0 copy-start.1
  127.1 10.6 %fusion.4 = f32[1024,512]{1,0:T(8,128)} fusion(bf16[1024,4096]{0,1:T(8,128)(2,1)} %all-gather.2.cloned.1.call-done, bf16[4096,512]{1,0:T(8,128)(2,1)} %param.6), kind=kOutput, calls=%fused_computation.5 | convolution fusion | flops 4294967296 | bytes 14680064 | tf_op jit(solution)/shard_map/dot_general | solution.py:10
  137.7 0.0 copy-done
  137.7 0.0 copy-done.1
  137.7 5.8 fusion.3
  143.5 0.0 all-reduce.3.cloned.1.call-update
  143.5 0.0 reduce-scatter.2.cloned.1.call-start
  143.6 157.9 %all-reduce.3.cloned.1.call-done = (f32[1024,512]{1,0:T(8,128)}, f32[1024,512]{1,0:T(8,128)}) async-done(((f32[1024,512]{1,0:T(8,128)}, f32[1024,512]{1,0:T(8,128)}), (f32[1024,512]{1,0:T(8,128)}, f32[1024,512]{1,0:T(8,128)})) %all-reduce.3.cloned.1.call-update) | async-done | bytes 4194320 | tf_op jit(solution)/shard_map/psum | solution.py:11
  301.5 13.7 %fusion = f32[1024,4096]{1,0:T(8,128)} fusion(bf16[512,4096]{1,0:T(8,128)(2,1)} %param.7, f32[1024,512]{1,0:T(8,128)} %get-tuple-element.5, f32[1024,512]{1,0:T(8,128)} %get-tuple-element.6), kind=kOutput, calls=%fused_computation.1 | convolution fusion | flops 4298113024 | bytes 25165824 | tf_op jit(solution)/shard_map/dot_general | solution.py:13
  315.2 0.0 reduce-scatter.2.cloned.1.call-update
  315.2 315.7 %reduce-scatter.2.cloned.1.call-done = f32[16,4096]{1,0:T(8,128)} async-done(((f32[1024,4096]{1,0:T(8,128)}), f32[16,4096]{1,0:T(8,128)}) %reduce-scatter.2.cloned.1.call-update) | async-done | bytes 262160 | tf_op jit(solution)/shard_map/reduce_scatter | solution.py:14
  631.0 1.6 convert_element_type.7
Async XLA Ops:
  6.5 120.5 %all-gather.2.cloned.1.call-start = ((), (), s32[]{:S(2)}) async-start(), calls=%async_computation.1 | async-start | bytes 8519680 | tf_op jit(solution)/shard_map/all_gather | solution.py:8
  7.3 294.2 %all-reduce.3.cloned.1.call-start = ((), (), s32[]{:S(2)}) async-start(), calls=%async_computation.3 | async-start | bytes 8388608 | tf_op jit(solution)/shard_map/psum | solution.py:11
  127.1 10.6 %copy-start = (bf16[1024,4096]{0,1:T(8,128)(2,1)S(1)}, bf16[1024,4096]{0,1:T(8,128)(2,1)}, u32[]{:S(2)}) copy-start(bf16[1024,4096]{0,1:T(8,128)(2,1)} %all-gather.2.cloned.1.call-done) | copy-start | bytes 25165828
  127.1 10.6 %copy-start.1 = (bf16[4096,512]{1,0:T(8,128)(2,1)S(1)}, bf16[4096,512]{1,0:T(8,128)(2,1)}, u32[]{:S(2)}) copy-start(bf16[4096,512]{1,0:T(8,128)(2,1)} %param.5) | copy-start | bytes 12582916
  143.5 487.4 %reduce-scatter.2.cloned.1.call-start = ((), (), s32[]{:S(2)}) async-start(), calls=%async_computation.2 | async-start | bytes 17039360 | tf_op jit(solution)/shard_map/reduce_scatter | solution.py:14
Sparse Core Ops, SparseCore 0:
  9.2 117.7 all-gather.1
  143.7 157.7 all-reduce.2
  315.4 315.5 reduce-scatter.1
where the time goes:
time: 643 us; the launch traced here: 639 us
  waiting for transfers between devices  594 us (92%)
  matrix products  30.2 us (5%)
  between operations  13.1 us (2%)
    reduce_scatter x1, waiting for transfers between devices, local(): mixed = lax.psum_scatter(terms, 'gy', scatter_dimension=0, tiled=True)  316 us
    psum x1, waiting for transfers between devices, local(): gate, up = lax.psum((gate_next, up_next), 'gx')  158 us
    all_gather x1, waiting for transfers between devices, local(): piece = lax.all_gather(tokens, 'gy', axis=1, tiled=True)  120 us
    dot_general x1, matrix products, local(): terms = jnp.dot(hidden, down_weight, preferred_element_type=jnp.float32)  13.7 us
  transfers between devices with their start and end apart: 3, of which 3 were waited for; matrix products, arithmetic and copies ran while one was open for 0% of the time, Pallas kernels for 0%

commit v1 on v0

v1 whole, which is shorter than its diff:
```python
import functools

import jax
import jax.numpy as jnp
from jax import lax
from jax.experimental import pallas as pl
from jax.experimental.pallas import tpu as pltpu
from jax.sharding import PartitionSpec as P

MESH = pl.DeviceIdType.MESH
F32, BF16 = jnp.float32, jnp.bfloat16
BLOCKS = 4
RING_TOKENS = False
RING_MIXED = False
MAX_SEMS = 320


def schedule(chain, gap):
    order = []
    for slot in range(len(chain) + gap * (BLOCKS - 1)):
        for b in range(BLOCKS):
            at = slot - gap * b
            if 0 <= at < len(chain):
                order.append((chain[at], b))
    return order


def kernel(
    tok_ref, wg_hbm, wu_hbm, wd_hbm, out_ref,
    wg, wu, wd, twin, twin_in, feats, part, zs, zr, hid, xs, xr, mix,
    as1, ar1, bs1, br1, aq, bq, as2, ar2, bs2, br2, res, pair_in, fin, fin_in,
    load_sem, send_sem, recv_sem,
):
    k, j = lax.axis_index("gx"), lax.axis_index("gy")
    c, x, l, y = j % 2, (j // 2) % 4, (j // 8) % 2, j // 16

    def gy(y, l, x, c):
        return ((y * 2 + l) * 4 + x) * 2 + c

    def at_x(d):
        return (k, gy(y, l, (x + d) % 4, c))

    def at_y(d):
        return (k, gy((y + d) % 4, l, x, c))

    def at_k(d):
        return ((k + d) % 4, j)

    sibling = (k, gy(y, l, x, 1 - c))
    partner = (k, gy(y, 1 - l, x, c))
    where = {"x": at_x, "y": at_y, "k": at_k}
    mine = {"x": x, "y": y, "k": k}

    loads = []
    for n, (src, dst) in enumerate(((wg_hbm, wg), (wu_hbm, wu), (wd_hbm, wd))):
        copy = pltpu.make_async_copy(src, dst, load_sem.at[n])
        copy.start()
        loads.append(copy)

    barrier = pltpu.get_barrier_semaphore()
    peers = [sibling, partner]
    peers += [at(d) for at in (at_x, at_y) for d in (1, 3, 2)]
    peers += [at_k(1), at_k(3)]
    for peer in peers:
        pl.semaphore_signal(barrier, inc=1, device_id=peer, device_id_type=MESH)

    sent = []

    def send(src, dst, to):
        n = len(sent)
        copy = pltpu.make_async_remote_copy(
            src_ref=src, dst_ref=dst, send_sem=send_sem.at[n], recv_sem=recv_sem.at[n],
            device_id=to, device_id_type=MESH,
        )
        copy.start()
        sent.append(copy)
        return copy

    for b in range(BLOCKS):
        for row in range(4):
            for col in range(4):
                first = row * 256 + (b % 2) * 128 + col * 32 + (b // 2) * 16
                v = tok_ref[first : first + 16, :]
                twin[b, row // 2, row % 2, col * 16 : col * 16 + 16, :] = jnp.concatenate([v, v], axis=1)

    pl.semaphore_wait(barrier, len(peers))
    first_swap = send(twin.at[:, 1 - c], twin_in, sibling)
    state = {}

    def ring_gather(key, axis, own, part_of, ring):
        m, at = mine[axis], where[axis]

        def start():
            s = own(m)
            state[key] = [send(s, s, at(1)), send(s, s, at(3))]
            if not ring:
                state[key].append(send(s, s, at(2)))

        def forward():
            left, right = state[key]
            left.wait_recv()
            s = part_of((m + 3) % 4, 0)
            on = [send(s, s, at(1))]
            right.wait_recv()
            s = part_of((m + 1) % 4, 1)
            on.append(send(s, s, at(3)))
            state[key] = on

        def done():
            for copy in state[key]:
                copy.wait_recv()

        return start, forward, done

    def scatter(key, axis, read, st, rc, ring):
        m, at = mine[axis], where[axis]

        def put(n, value):
            st[n] = value.astype(BF16)

        def start():
            opp, nxt, prv = (m + 2) % 4, (m + 1) % 4, (m + 3) % 4
            put(0, read(opp, 0))
            put(1, read(opp, 1))
            if ring:
                first = [send(st.at[0], rc.at[0], at(1)), send(st.at[1], rc.at[1], at(3))]
                put(2, read(nxt, 1))
                put(3, read(prv, 0))
                rest = [send(st.at[2], rc.at[2], at(1)), send(st.at[3], rc.at[3], at(3))]
                state[key] = (first, rest)
            else:
                rest = [send(st.at[pl.ds(0, 2)], rc.at[pl.ds(0, 2)], at(2))]
                for n, chunk, d in ((2, nxt, 1), (4, prv, 3)):
                    put(n, read(chunk, 0))
                    put(n + 1, read(chunk, 1))
                    rest.append(send(st.at[pl.ds(n, 2)], rc.at[pl.ds(n, 2)], at(d)))
                state[key] = ((), rest)

        def forward():
            first, rest = state[key]
            first[0].wait_recv()
            put(4, read((m + 1) % 4, 0) + rc[0].astype(F32))
            rest.append(send(st.at[4], rc.at[4], at(1)))
            first[1].wait_recv()
            put(5, read((m + 3) % 4, 1) + rc[1].astype(F32))
            rest.append(send(st.at[5], rc.at[5], at(3)))

        def done():
            for copy in state[key][1]:
                copy.wait_recv()

        def total(h):
            if ring:
                terms = (3, 4) if h == 0 else (2, 5)
            else:
                terms = (h, 2 + h, 4 + h)
            value = read(m, h)
            for n in terms:
                value = value + rc[n].astype(F32)
            return value

        return start, forward, done, total

    steps = {}

    def step(name):
        def add(f):
            steps[name] = f
            return f

        return add

    @step("pair")
    def _(b):
        if b == 0:
            first_swap.wait_recv()
        own = twin[b, c].reshape(128, 128)
        other = twin_in[b].reshape(128, 128)
        lane = lax.broadcasted_iota(jnp.int32, (128, 128), 1)
        low = jnp.where(lane < 64, 0, 1) == c
        block = jnp.where(low, own.astype(F32), other.astype(F32)).astype(BF16)
        feats[y, l, x, b, c] = block.reshape(2, 64, 128)
        s = feats.at[y, l, x, b, c]
        state["pair", b] = send(s, s, partner)

    def gathers(b):
        near = [
            ring_gather(("nx", b), "x", lambda m: feats.at[y, :, m, b, c, 0],
                        lambda m, h: feats.at[y, h, m, b, c, 0], RING_TOKENS),
            ring_gather(("ny", b), "y", lambda m: feats.at[m, :, x, b, c, 1],
                        lambda m, h: feats.at[m, h, x, b, c, 1], RING_TOKENS),
        ]
        far = [
            ring_gather(("fy", b), "y", lambda m: feats.at[m, :, :, b, c, 0],
                        lambda m, h: feats.at[m, h, :, b, c, 0], RING_TOKENS),
            ring_gather(("fx", b), "x", lambda m: feats.at[:, :, m, b, c, 1],
                        lambda m, h: feats.at[:, h, m, b, c, 1], RING_TOKENS),
        ]
        return near, far

    def to_sibling(b, d, which):
        s = feats.at[(y + d) % 4, :, :, b, c, 0] if which == 0 else feats.at[:, :, (x + d) % 4, b, c, 1]
        state.setdefault(("sib", b), []).append(send(s, s, sibling))

    @step("near")
    def _(b):
        state["pair", b].wait_recv()
        for g in gathers(b)[0]:
            g[0]()

    if RING_TOKENS:

        @step("near on")
        def _(b):
            for g in gathers(b)[0]:
                g[1]()

    @step("far")
    def _(b):
        near, far = gathers(b)
        for n in range(2):
            near[n][2]()
            far[n][0]()
        for n in range(2):
            to_sibling(b, 0, n)

    if RING_TOKENS:

        @step("far on")
        def _(b):
            for n, g in enumerate(gathers(b)[1]):
                g[1]()
                to_sibling(b, 1, n)
                to_sibling(b, 3, n)

        @step("far end")
        def _(b):
            for n, g in enumerate(gathers(b)[1]):
                g[2]()
                to_sibling(b, 2, n)
    else:

        @step("far end")
        def _(b):
            for n, d in enumerate((3, 1, 2)):
                for which, key in enumerate(("fy", "fx")):
                    state[key, b][n].wait_recv()
                    to_sibling(b, d, which)

    def z_read(b):
        return lambda chunk, h: part[b % 2, chunk, h * 32 : h * 32 + 32, :]

    @step("up")
    def _(b):
        for copy in state["sib", b]:
            copy.wait_recv()
        if b == 0:
            loads[0].wait()
            loads[1].wait()
        for which, w in enumerate((wg, wu)):

            @pl.loop(0, 2)
            def _(n):
                lhs = jnp.concatenate(
                    [feats[s // 8, s // 4 % 2, s % 4, b].reshape(256, 128) for s in range(32)], axis=1
                )
                cols = pl.ds(pl.multiple_of(n * 256, 256), 256)
                got = jnp.dot(lhs, w[:, cols], preferred_element_type=F32)
                at = pl.ds(pl.multiple_of(which * 512 + n * 256, 256), 256)
                part[b % 2, :, :, at] = got.reshape(4, 64, 256)

        state["z", b] = scatter(("zs", b), "k", z_read(b), zs.at[b], zr.at[b], True)
        state["z", b][0]()

    @step("z on")
    def _(b):
        state["z", b][1]()

    def h_gather(b):
        return ring_gather(("h", b), "k", lambda m: hid.at[b, m], lambda m, h: hid.at[b, m, pl.ds(h * 32, 32)], True)

    @step("act")
    def _(b):
        _, _, done, total = state["z", b]
        done()
        for h in range(2):
            both = total(h)
            gate, up = both[:, :512], both[:, 512:]
            value = gate / (1.0 + jnp.exp(-gate)) * up
            hid[b, k, h * 32 : h * 32 + 32, :] = value.astype(BF16)
        h_gather(b)[0]()

    @step("h on")
    def _(b):
        h_gather(b)[1]()

    @step("down")
    def _(b):
        h_gather(b)[2]()
        if b == 0:
            loads[2].wait()

        def tile(half, n):
            cols = pl.ds(pl.multiple_of(half * 2048 + n * 512, 512), 512)
            got = jnp.dot(hid[b].reshape(256, 512), wd[:, cols], preferred_element_type=F32)
            return got.reshape(4, 4, 16, 512)

        @pl.loop(0, 4)
        def _(n):
            xs[b, :, :, :, pl.ds(pl.multiple_of(n * 512, 512), 512)] = tile(1 - c, n).astype(BF16)

        state["swap", b] = send(xs.at[b], xr.at[b], sibling)

        @pl.loop(0, 4)
        def _(n):
            mix[b, :, :, :, pl.ds(pl.multiple_of(n * 512, 512), 512)] = tile(c, n)

    @step("mix")
    def _(b):
        state["swap", b].wait_recv()

        @pl.loop(0, 4)
        def _(n):
            mix[b, n] = mix[b, n] + xr[b, n].astype(F32)

        a = scatter(("a1", b), "y", lambda ch, h: mix[b, ch, 2 * h : 2 * h + 2, :, :1024],
                    as1.at[b], ar1.at[b], RING_MIXED)
        v = scatter(("b1", b), "x", lambda ch, h: mix[b, 2 * h : 2 * h + 2, ch, :, 1024:],
                    bs1.at[b], br1.at[b], RING_MIXED)
        state["m1", b] = (a, v)
        a[0]()
        v[0]()

    if RING_MIXED:

        @step("mix on")
        def _(b):
            for s in state["m1", b]:
                s[1]()

    @step("mix end")
    def _(b):
        for (_, _, done, total), q in zip(state["m1", b], (aq, bq)):
            done()
            for h in range(2):
                q[b, 2 * h : 2 * h + 2] = total(h)
        a = scatter(("a2", b), "x", lambda ch, h: aq[b, ch, :, h * 512 : h * 512 + 512],
                    as2.at[b], ar2.at[b], RING_MIXED)
        v = scatter(("b2", b), "y", lambda ch, h: bq[b, ch, :, h * 512 : h * 512 + 512],
                    bs2.at[b], br2.at[b], RING_MIXED)
        state["m2", b] = (a, v)
        a[0]()
        v[0]()

    if RING_MIXED:

        @step("rest on")
        def _(b):
            for s in state["m2", b]:
                s[1]()

    @step("rest end")
    def _(b):
        for n, (_, _, done, total) in enumerate(state["m2", b]):
            done()
            for h in range(2):
                res[b, :, n * 1024 + h * 512 : n * 1024 + h * 512 + 512] = total(h)
        if b % 2 == 1:
            p = b // 2
            state["low", p] = send(res.at[2 * p + (1 - l)], pair_in.at[p], partner)

    @step("low")
    def _(b):
        if b % 2 == 1:
            p = b // 2
            state["low", p].wait_recv()
            fin[p] = (res[2 * p + l] + pair_in[p]).astype(BF16)

    for name, b in schedule(list(steps), 2):
        steps[name](b)

    last = send(fin.at[1 - c], fin_in, sibling)
    out_ref[:, pl.ds(pl.multiple_of(c * 2048, 2048), 2048)] = fin[c]
    last.wait_recv()
    out_ref[:, pl.ds(pl.multiple_of((1 - c) * 2048, 2048), 2048)] = fin_in[...]
    for copy in sent:
        copy.wait_send()
    assert len(sent) <= MAX_SEMS


def local(tokens, gate_weight, up_weight, down_weight):
    n = BLOCKS
    scratch = [
        pltpu.VMEM((4096, 512), BF16),
        pltpu.VMEM((4096, 512), BF16),
        pltpu.VMEM((512, 4096), BF16),
        pltpu.VMEM((n, 2, 2, 64, 128), BF16),
        pltpu.VMEM((n, 2, 64, 128), BF16),
        pltpu.VMEM((4, 2, 4, n, 2, 2, 64, 128), BF16),
        pltpu.VMEM((2, 4, 64, 1024), F32),
        pltpu.VMEM((n, 6, 32, 1024), BF16),
        pltpu.VMEM((n, 6, 32, 1024), BF16),
        pltpu.VMEM((n, 4, 64, 512), BF16),
        pltpu.VMEM((n, 4, 4, 16, 2048), BF16),
        pltpu.VMEM((n, 4, 4, 16, 2048), BF16),
        pltpu.VMEM((n, 4, 4, 16, 2048), F32),
        *[pltpu.VMEM((n, 6, 2, 16, 1024), BF16) for _ in range(4)],
        *[pltpu.VMEM((n, 4, 16, 1024), F32) for _ in range(2)],
        *[pltpu.VMEM((n, 6, 16, 512), BF16) for _ in range(4)],
        pltpu.VMEM((n, 16, 2048), F32),
        pltpu.VMEM((2, 16, 2048), F32),
        pltpu.VMEM((2, 16, 2048), BF16),
        pltpu.VMEM((16, 2048), BF16),
        pltpu.SemaphoreType.DMA((3,)),
        pltpu.SemaphoreType.DMA((MAX_SEMS,)),
        pltpu.SemaphoreType.DMA((MAX_SEMS,)),
    ]
    return pl.pallas_call(
        kernel,
        name="swiglu_layer",
        out_shape=jax.ShapeDtypeStruct((16, 4096), BF16),
        in_specs=[pl.BlockSpec(memory_space=pltpu.VMEM)] + [pl.BlockSpec(memory_space=pl.ANY)] * 3,
        out_specs=pl.BlockSpec(memory_space=pltpu.VMEM),
        scratch_shapes=scratch,
        cost_estimate=pl.CostEstimate(flops=12_900_000_000, bytes_accessed=13_000_000, transcendentals=131072),
        compiler_params=pltpu.CompilerParams(
            collective_id=0, has_side_effects=True, vmem_limit_bytes=62 * 2**20
        ),
    )(tokens, gate_weight, up_weight, down_weight)


def solution(mesh):
    placed = (P(None, ("gx", "gy")), P("gx", "gy"), P("gx", "gy"), P("gy", "gx"))
    return jax.shard_map(local, mesh=mesh, in_specs=placed, out_specs=P("gy", "gx"), check_vma=False)
```

time: 643 us -> 135 us (0.21)
  waiting for transfers between devices: 594 us -> 0 us
  Pallas kernels: 0 us -> 131 us
  matrix products: 30.2 us -> 0 us
  between operations: 13.1 us -> 0.01 us
    reduce_scatter x1 -> x0, waiting for transfers between devices: 316 us -> none  [local(): mixed = lax.psum_scatter(terms, 'gy', scatter_dimension=0, tiled=True)]
    psum x1 -> x0, waiting for transfers between devices: 158 us -> none  [local(): gate, up = lax.psum((gate_next, up_next), 'gx')]
    pallas_call x0 -> x1, Pallas kernels: none -> 131 us  [local(): pl.pallas_call(kernel, name='swiglu_layer', out_shape=jax.ShapeDtypeStruc...]
    all_gather x1 -> x0, waiting for transfers between devices: 120 us -> none  [local(): piece = lax.all_gather(tokens, 'gy', axis=1, tiled=True)]
    dot_general x3 -> x0, matrix products: 30.2 us -> none  [the longest x1 13.7 us: local(): terms = jnp.dot(hidden, down_weight, preferred_element_type=jnp.float32)]
  transfers between devices with their start and end apart: 3 -> 0, of which waited for: 3 -> 0; matrix products, arithmetic and copies ran while one was open for 0% -> 0% of each run, Pallas kernels for 0% -> 0%
where the time goes in v1:
time: 135 us; the launch traced here: 134 us
  Pallas kernels  131 us (97%)
  local copies, waits for them, and re-layouts  3.3 us (2%)
    pallas_call x1, Pallas kernels, local(): pl.pallas_call(kernel, name='swiglu_layer', out_shape=jax.ShapeDtypeStruc...  131 us
    unnamed x2, local copies, waits for them, and re-layouts  3.3 us

profile of v1, /device:TPU:1, one launch (start us, length us, event | category | flops | bytes accessed | tf_op | source)
XLA Modules:
  0.0 134.5 jit_solution(11154994054825633427)
XLA Ops:
  0.0 1.7 %copy.5.tok_ref = bf16[1024,64]{1,0:T(8,128)(2,1)} copy(bf16[1024,64]{0,1:T(8,128)(2,1)} %param.4) | data formatting | bytes 262144 | tf_op args[0]
  1.7 131.2 %swiglu_layer.1 = bf16[16,4096]{1,0:T(8,128)(2,1)} custom-call(bf16[1024,64]{1,0:T(8,128)(2,1)} %copy.5.tok_ref, bf16[4096,512]{1,0:T(8,128)(2,1)} %wg_hbm.1, bf16[4096,512]{1,0:T(8,128)(2,1)} %wu_hbm.1, bf16[512,4096]{1,0:T(8,128)(2,1)} %wd_hbm.1), custom_call_target="tpu_custom_call" | custom-call | flops 12899999744 | bytes 13000000 | tf_op jit(solution)/shard_map/swiglu_layer/pallas_call | solution.py:418
  132.9 1.6 %copy.7 = bf16[16,4096]{1,0:T(8,128)(2,1)} copy(bf16[16,4096]{1,0:T(8,128)(2,1)} %swiglu_layer.1) | data formatting | bytes 262144

commit v2 on v0

v2 whole, which is shorter than its diff:
```python
import functools

import jax
import jax.numpy as jnp
from jax import lax
from jax.experimental import pallas as pl
from jax.experimental.pallas import tpu as pltpu
from jax.sharding import PartitionSpec as P

MESH = pl.DeviceIdType.MESH
F32, BF16 = jnp.float32, jnp.bfloat16
BLOCKS = 4
UNITS = 8
PER = UNITS // BLOCKS
ROWS = 1024 // UNITS
QUARTER = ROWS // 4
REST = F32
MAX_SEMS = 384

ORDER = (
    (0, 0), (0, 4), (0, 3), (0, 1), (0, 7), (1, 0), (1, 3), (1, 1), (1, 4), (2, 0), (2, 1), (0, 6),
    (2, 4), (0, 2), (1, 6), (3, 0), (4, 0), (2, 3), (1, 7), (1, 2), (3, 1), (4, 1), (5, 0), (5, 1),
    (3, 4), (3, 3), (2, 6), (6, 0), (4, 3), (2, 2), (0, 5), (6, 1), (5, 3), (7, 0), (1, 5), (3, 6),
    (7, 1), (3, 2), (4, 2), (4, 6), (6, 3), (4, 4), (2, 7), (5, 2), (5, 4), (3, 7), (2, 5), (6, 2),
    (4, 7), (8, 1), (8, 0), (5, 6), (3, 5), (4, 5), (7, 2), (7, 3), (9, 1), (5, 5), (9, 0), (6, 4),
    (8, 2), (10, 1), (8, 3), (6, 5), (5, 7), (10, 0), (7, 4), (9, 3), (9, 2), (7, 5), (6, 7), (10, 3),
    (11, 1), (6, 6), (8, 4), (10, 2), (8, 5), (7, 7), (11, 0), (7, 6), (9, 5), (11, 3), (8, 7), (9, 4),
    (8, 6), (10, 5), (10, 4), (9, 7), (9, 6), (10, 7), (10, 6), (11, 5), (11, 2), (11, 4), (12, 0), (12, 3),
    (12, 1), (11, 7), (11, 6), (12, 2), (13, 0), (12, 5), (12, 4), (12, 7), (12, 6), (13, 3), (13, 1), (14, 1),
    (13, 2), (14, 0),
)

def kernel(
    tok_ref, wg_hbm, wu_hbm, wd_hbm, out_ref,
    wg, wu, wd, twin, twin_in, feats, part, zs, zr, hid, xs, xr, mix,
    s1, r1, q1, s2, r2, res, pair_in, fin, fin_in,
    load_sem, send_sem, recv_sem,
):
    k, j = lax.axis_index("gx"), lax.axis_index("gy")
    c, x, l, y = j % 2, (j // 2) % 4, (j // 8) % 2, j // 16

    def gy(y, l, x, c):
        return ((y * 2 + l) * 4 + x) * 2 + c

    def at_x(d):
        return (k, gy(y, l, (x + d) % 4, c))

    def at_y(d):
        return (k, gy((y + d) % 4, l, x, c))

    def at_k(d):
        return ((k + d) % 4, j)

    sibling = (k, gy(y, l, x, 1 - c))
    partner = (k, gy(y, 1 - l, x, c))
    where = {"x": at_x, "y": at_y, "k": at_k}
    mine = {"x": x, "y": y, "k": k}

    loads = []
    for n, (src, dst) in enumerate(((wg_hbm, wg), (wu_hbm, wu), (wd_hbm, wd))):
        copy = pltpu.make_async_copy(src, dst, load_sem.at[n])
        copy.start()
        loads.append(copy)

    barrier = pltpu.get_barrier_semaphore()
    peers = [sibling, partner]
    peers += [at(d) for at in (at_x, at_y) for d in (1, 3, 2)]
    peers += [at_k(1), at_k(3)]
    for peer in peers:
        pl.semaphore_signal(barrier, inc=1, device_id=peer, device_id_type=MESH)

    sent = []

    def send(src, dst, to):
        n = len(sent)
        copy = pltpu.make_async_remote_copy(
            src_ref=src, dst_ref=dst, send_sem=send_sem.at[n], recv_sem=recv_sem.at[n],
            device_id=to, device_id_type=MESH,
        )
        copy.start()
        sent.append(copy)
        return copy

    for b in range(BLOCKS):
        for group in range(16):
            first = group // 4 * 256 + (b % 2) * 128 + group % 4 * 32 + (b // 2) * 16
            v = tok_ref[first : first + 16, :]
            at = b * 256 + group * 16
            u, row = at // ROWS, at % ROWS
            twin[u, row // (2 * QUARTER), row % (2 * QUARTER) : row % (2 * QUARTER) + 16, :] = jnp.concatenate(
                [v, v], axis=1
            )

    pl.semaphore_wait(barrier, len(peers))
    first_swap = send(twin.at[:, 1 - c], twin_in, sibling)
    state = {}

    def gather(key, axis, own):
        at = where[axis]

        def start():
            s = own(mine[axis])
            state[key] = [send(s, s, at(1)), send(s, s, at(3)), send(s, s, at(2))]

        def done():
            once(state[key])

        return start, done

    def ring_gather(key, own, part_of):
        def start():
            s = own(k)
            state[key] = [send(s, s, at_k(1)), send(s, s, at_k(3))]

        def forward():
            left, right = state[key]
            left.wait_recv()
            s = part_of((k + 3) % 4, 0)
            on = [send(s, s, at_k(1))]
            right.wait_recv()
            s = part_of((k + 1) % 4, 1)
            on.append(send(s, s, at_k(3)))
            state[key] = on

        return start, forward

    def scatter(key, axis, read, st, rc):
        m, at = mine[axis], where[axis]

        def start():
            copies = []
            for n, d in enumerate((2, 1, 3)):
                st[n] = read((m + d) % 4).astype(st.dtype)
                copies.append(send(st.at[n], rc.at[n], at(d)))
            state[key] = copies

        def done():
            value = read(m)
            for n in (1, 2, 0):
                state[key][n].wait_recv()
                value = value + rc[n].astype(F32)
            return value

        return start, done

    def ring_scatter(key, read, st, rc):
        def put(n, value):
            st[n] = value.astype(BF16)

        def start():
            opp, nxt, prv = (k + 2) % 4, (k + 1) % 4, (k + 3) % 4
            put(0, read(opp, 0))
            put(1, read(opp, 1))
            first = [send(st.at[0], rc.at[0], at_k(1)), send(st.at[1], rc.at[1], at_k(3))]
            put(2, read(nxt, 1))
            put(3, read(prv, 0))
            rest = [send(st.at[2], rc.at[2], at_k(1)), send(st.at[3], rc.at[3], at_k(3))]
            state[key] = (first, rest)

        def forward():
            first, rest = state[key]
            first[0].wait_recv()
            put(4, read((k + 1) % 4, 0) + rc[0].astype(F32))
            rest.append(send(st.at[4], rc.at[4], at_k(1)))
            first[1].wait_recv()
            put(5, read((k + 3) % 4, 1) + rc[1].astype(F32))
            rest.append(send(st.at[5], rc.at[5], at_k(3)))

        def done():
            once(state[key][1])

        def total(h):
            value = read(k, h)
            for n in (3, 4) if h == 0 else (2, 5):
                value = value + rc[n].astype(F32)
            return value

        return start, forward, done, total

    def once(copies):
        for copy in copies:
            copy.wait_recv()
        copies.clear()

    swap_in, weights_in, down_in = [first_swap], loads[:2], loads[2:]

    def pair(u):
        once(swap_in)
        own, other = twin[u, c], twin_in[u]
        lane = lax.broadcasted_iota(jnp.int32, own.shape, 1)
        low = jnp.where(lane < 64, 0, 1) == c
        block = jnp.where(low, own.astype(F32), other.astype(F32)).astype(BF16)
        feats[y, l, x, u, c] = block.reshape(2, QUARTER, 128)
        s = feats.at[y, l, x, u, c]
        state["pair", u] = send(s, s, partner)

    def gathers(u):
        near = [
            gather(("nx", u), "x", lambda m: feats.at[y, :, m, u, c, 0]),
            gather(("ny", u), "y", lambda m: feats.at[m, :, x, u, c, 1]),
        ]
        far = [
            gather(("fy", u), "y", lambda m: feats.at[m, :, :, u, c, 0]),
            gather(("fx", u), "x", lambda m: feats.at[:, :, m, u, c, 1]),
        ]
        return near, far

    def to_sibling(u, d, which):
        s = feats.at[(y + d) % 4, :, :, u, c, 0] if which == 0 else feats.at[:, :, (x + d) % 4, u, c, 1]
        state.setdefault(("sib", u), []).append(send(s, s, sibling))

    def near(u):
        state["pair", u].wait_recv()
        for g in gathers(u)[0]:
            g[0]()

    def far(u):
        near, far = gathers(u)
        for n in range(2):
            near[n][1]()
            far[n][0]()
        for n in range(2):
            to_sibling(u, 0, n)

    def far_mid(u):
        for which, key in enumerate(("fy", "fx")):
            for n, d in ((0, 3), (1, 1)):
                state[key, u][n].wait_recv()
                to_sibling(u, d, which)

    def far_end(u):
        for which, key in enumerate(("fy", "fx")):
            state[key, u][2].wait_recv()
            to_sibling(u, 2, which)

    def up(u):
        once(state["sib", u])
        while weights_in:
            weights_in.pop().wait()
        for which, w in enumerate((wg, wu)):

            @pl.loop(0, 2)
            def _(n):
                lhs = jnp.concatenate(
                    [feats[s // 8, s // 4 % 2, s % 4, u].reshape(ROWS, 128) for s in range(32)], axis=1
                )
                cols = pl.ds(pl.multiple_of(n * 256, 256), 256)
                got = jnp.dot(lhs, w[:, cols], preferred_element_type=F32)
                at = pl.ds(pl.multiple_of(which * 512 + n * 256, 256), 256)
                part[u, :, :, at] = got.reshape(4, QUARTER, 256)

        half = QUARTER // 2
        state["z", u] = ring_scatter(
            ("zs", u), lambda chunk, h: part[u, chunk, h * half : h * half + half, :], zs.at[u], zr.at[u]
        )
        state["z", u][0]()

    def z_on(u):
        state["z", u][1]()

    def h_gather(u):
        half = QUARTER // 2
        return ring_gather(("h", u), lambda m: hid.at[u, m], lambda m, h: hid.at[u, m, pl.ds(h * half, half)])

    def act(u):
        _, _, done, total = state["z", u]
        done()
        half = QUARTER // 2
        for h in range(2):
            both = total(h)
            gate, up = both[:, :512], both[:, 512:]
            value = gate / (1.0 + jnp.exp(-gate)) * up
            hid[u, k, h * half : h * half + half, :] = value.astype(BF16)
        h_gather(u)[0]()

    def h_on(u):
        h_gather(u)[1]()

    def down(i):
        b, p = i // 2, i % 2
        for u in range(b * PER, b * PER + PER):
            once(state["h", u])
        while down_in:
            down_in.pop().wait()

        def tile(half, n):
            cols = pl.ds(pl.multiple_of(half * 2048 + p * 1024 + n * 512, 512), 512)
            got = jnp.dot(hid[b * PER : b * PER + PER].reshape(256, 512), wd[:, cols], preferred_element_type=F32)
            return got.reshape(4, 4, 16, 512)

        @pl.loop(0, 2)
        def _(n):
            xs[i, :, :, :, pl.ds(pl.multiple_of(n * 512, 512), 512)] = tile(1 - c, n).astype(xs.dtype)

        state["swap", i] = send(xs.at[i], xr.at[i], sibling)

        @pl.loop(0, 2)
        def _(n):
            mix[i, :, :, :, pl.ds(pl.multiple_of(n * 512, 512), 512)] = tile(c, n)

    def mixed(i):
        state["swap", i].wait_recv()
        if i % 2 == 0:
            read = lambda m: mix[i, m] + xr[i, m].astype(F32)
        else:
            read = lambda m: mix[i, :, m] + xr[i, :, m].astype(F32)
        state["m1", i] = scatter(("first", i), "yx"[i % 2], read, s1.at[i], r1.at[i])
        state["m1", i][0]()

    def mixed_end(i):
        q1[i] = state["m1", i][1]()
        state["m2", i] = scatter(("second", i), "xy"[i % 2], lambda m: q1[i, m], s2.at[i], r2.at[i])
        state["m2", i][0]()

    def rest_end(i):
        b, p = i // 2, i % 2
        res[b, p] = state["m2", i][1]()
        q = b // 2
        state["rest", q, p] = state.get(("rest", q, p), 0) + 1
        if state["rest", q, p] == 2:
            state["low", q, p] = send(res.at[2 * q + (1 - l), p], pair_in.at[q, p], partner)

    def low(i):
        q, p = i // 2, i % 2
        state["low", q, p].wait_recv()
        fin[q, p] = (res[2 * q + l, p] + pair_in[q, p]).astype(BF16)

    def last(p):
        state["last", p] = send(fin.at[1 - c, p], fin_in.at[p], sibling)
        out_ref[:, pl.ds(pl.multiple_of(c * 2048 + p * 1024, 1024), 1024)] = fin[c, p]

    steps = (pair, near, far, far_mid, far_end, up, z_on, act, h_on, down, mixed, mixed_end, rest_end, low, last)
    for n, i in ORDER:
        steps[n](i)
    for p in range(2):
        state["last", p].wait_recv()
        out_ref[:, pl.ds(pl.multiple_of((1 - c) * 2048 + p * 1024, 1024), 1024)] = fin_in[p]
    for copy in sent:
        copy.wait_send()
    assert len(sent) <= MAX_SEMS


def local(tokens, gate_weight, up_weight, down_weight):
    scratch = [
        pltpu.VMEM((4096, 512), BF16),
        pltpu.VMEM((4096, 512), BF16),
        pltpu.VMEM((512, 4096), BF16),
        pltpu.VMEM((UNITS, 2, 2 * QUARTER, 128), BF16),
        pltpu.VMEM((UNITS, 2 * QUARTER, 128), BF16),
        pltpu.VMEM((4, 2, 4, UNITS, 2, 2, QUARTER, 128), BF16),
        pltpu.VMEM((UNITS, 4, QUARTER, 1024), F32),
        pltpu.VMEM((UNITS, 6, QUARTER // 2, 1024), BF16),
        pltpu.VMEM((UNITS, 6, QUARTER // 2, 1024), BF16),
        pltpu.VMEM((UNITS, 4, QUARTER, 512), BF16),
        pltpu.VMEM((2 * BLOCKS, 4, 4, 16, 1024), BF16),
        pltpu.VMEM((2 * BLOCKS, 4, 4, 16, 1024), BF16),
        pltpu.VMEM((2 * BLOCKS, 4, 4, 16, 1024), F32),
        pltpu.VMEM((2 * BLOCKS, 3, 4, 16, 1024), BF16),
        pltpu.VMEM((2 * BLOCKS, 3, 4, 16, 1024), BF16),
        pltpu.VMEM((2 * BLOCKS, 4, 16, 1024), F32),
        pltpu.VMEM((2 * BLOCKS, 3, 16, 1024), REST),
        pltpu.VMEM((2 * BLOCKS, 3, 16, 1024), REST),
        pltpu.VMEM((BLOCKS, 2, 16, 1024), F32),
        pltpu.VMEM((2, 2, 16, 1024), F32),
        pltpu.VMEM((2, 2, 16, 1024), BF16),
        pltpu.VMEM((2, 16, 1024), BF16),
        pltpu.SemaphoreType.DMA((3,)),
        pltpu.SemaphoreType.DMA((MAX_SEMS,)),
        pltpu.SemaphoreType.DMA((MAX_SEMS,)),
    ]
    return pl.pallas_call(
        kernel,
        name="swiglu_layer",
        out_shape=jax.ShapeDtypeStruct((16, 4096), BF16),
        in_specs=[pl.BlockSpec(memory_space=pltpu.VMEM)] + [pl.BlockSpec(memory_space=pl.ANY)] * 3,
        out_specs=pl.BlockSpec(memory_space=pltpu.VMEM),
        scratch_shapes=scratch,
        cost_estimate=pl.CostEstimate(flops=12_900_000_000, bytes_accessed=13_000_000, transcendentals=131072),
        compiler_params=pltpu.CompilerParams(
            collective_id=0, has_side_effects=True, vmem_limit_bytes=62 * 2**20
        ),
    )(tokens, gate_weight, up_weight, down_weight)


def solution(mesh):
    placed = (P(None, ("gx", "gy")), P("gx", "gy"), P("gx", "gy"), P("gy", "gx"))
    return jax.shard_map(local, mesh=mesh, in_specs=placed, out_specs=P("gy", "gx"), check_vma=False)
```

time: 643 us -> 124 us (0.19)
  waiting for transfers between devices: 594 us -> 0 us
  Pallas kernels: 0 us -> 120 us
  matrix products: 30.2 us -> 0 us
  between operations: 13.1 us -> 0.01 us
    reduce_scatter x1 -> x0, waiting for transfers between devices: 316 us -> none  [local(): mixed = lax.psum_scatter(terms, 'gy', scatter_dimension=0, tiled=True)]
    psum x1 -> x0, waiting for transfers between devices: 158 us -> none  [local(): gate, up = lax.psum((gate_next, up_next), 'gx')]
    pallas_call x0 -> x1, Pallas kernels: none -> 120 us  [local(): pl.pallas_call(kernel, name='swiglu_layer', out_shape=jax.ShapeDtypeStruc...]
    all_gather x1 -> x0, waiting for transfers between devices: 120 us -> none  [local(): piece = lax.all_gather(tokens, 'gy', axis=1, tiled=True)]
    dot_general x3 -> x0, matrix products: 30.2 us -> none  [the longest x1 13.7 us: local(): terms = jnp.dot(hidden, down_weight, preferred_element_type=jnp.float32)]
  transfers between devices with their start and end apart: 3 -> 0, of which waited for: 3 -> 0; matrix products, arithmetic and copies ran while one was open for 0% -> 0% of each run, Pallas kernels for 0% -> 0%
where the time goes in v2:
time: 124 us
  Pallas kernels  120 us (97%)
  local copies, waits for them, and re-layouts  3.3 us (3%)
    pallas_call x1, Pallas kernels, local(): pl.pallas_call(kernel, name='swiglu_layer', out_shape=jax.ShapeDtypeStruc...  120 us
    unnamed x2, local copies, waits for them, and re-layouts  3.3 us

profile of v2, /device:TPU:1, one launch (start us, length us, event | category | flops | bytes accessed | tf_op | source)
XLA Modules:
  0.0 123.7 jit_solution(233177582804782923)
XLA Ops:
  0.0 1.7 %copy.5.tok_ref = bf16[1024,64]{1,0:T(8,128)(2,1)} copy(bf16[1024,64]{0,1:T(8,128)(2,1)} %param.4) | data formatting | bytes 262144 | tf_op args[0]
  1.7 120.3 %swiglu_layer.1 = bf16[16,4096]{1,0:T(8,128)(2,1)} custom-call(bf16[1024,64]{1,0:T(8,128)(2,1)} %copy.5.tok_ref, bf16[4096,512]{1,0:T(8,128)(2,1)} %wg_hbm.1, bf16[4096,512]{1,0:T(8,128)(2,1)} %wu_hbm.1, bf16[512,4096]{1,0:T(8,128)(2,1)} %wd_hbm.1), custom_call_target="tpu_custom_call" | custom-call | flops 12899999744 | bytes 13000000 | tf_op jit(solution)/shard_map/swiglu_layer/pallas_call | solution.py:371
  122.1 1.6 %copy.7 = bf16[16,4096]{1,0:T(8,128)(2,1)} copy(bf16[16,4096]{1,0:T(8,128)(2,1)} %swiglu_layer.1) | data formatting | bytes 262144

commit v3 on v2

--- a/solution.py
+++ b/solution.py
@@ -26,14 +26,14 @@
     (8, 2), (10, 1), (8, 3), (6, 5), (5, 7), (10, 0), (7, 4), (9, 3), (9, 2), (7, 5), (6, 7), (10, 3),
     (11, 1), (6, 6), (8, 4), (10, 2), (8, 5), (7, 7), (11, 0), (7, 6), (9, 5), (11, 3), (8, 7), (9, 4),
     (8, 6), (10, 5), (10, 4), (9, 7), (9, 6), (10, 7), (10, 6), (11, 5), (11, 2), (11, 4), (12, 0), (12, 3),
-    (12, 1), (11, 7), (11, 6), (12, 2), (13, 0), (12, 5), (12, 4), (12, 7), (12, 6), (13, 3), (13, 1), (14, 1),
-    (13, 2), (14, 0),
+    (12, 1), (11, 7), (11, 6), (12, 2), (13, 0), (12, 5), (12, 4), (12, 7), (12, 6), (13, 3), (13, 1),
+    (13, 2),
 )
 
 def kernel(
     tok_ref, wg_hbm, wu_hbm, wd_hbm, out_ref,
     wg, wu, wd, twin, twin_in, feats, part, zs, zr, hid, xs, xr, mix,
-    s1, r1, q1, s2, r2, res, pair_in, fin, fin_in,
+    s1, r1, q1, s2, r2, res, ends,
     load_sem, send_sem, recv_sem,
 ):
     k, j = lax.axis_index("gx"), lax.axis_index("gy")
@@ -63,7 +63,7 @@
         loads.append(copy)
 
     barrier = pltpu.get_barrier_semaphore()
-    peers = [sibling, partner]
+    peers = [sibling, partner, (k, gy(y, 1 - l, x, 1 - c))]
     peers += [at(d) for at in (at_x, at_y) for d in (1, 3, 2)]
     peers += [at_k(1), at_k(3)]
     for peer in peers:
@@ -78,18 +78,21 @@
             device_id=to, device_id_type=MESH,
         )
         copy.start()
-        sent.append(copy)
+        sent.append(copy.wait_send)
         return copy
 
-    for b in range(BLOCKS):
-        for group in range(16):
-            first = group // 4 * 256 + (b % 2) * 128 + group % 4 * 32 + (b // 2) * 16
-            v = tok_ref[first : first + 16, :]
-            at = b * 256 + group * 16
-            u, row = at // ROWS, at % ROWS
-            twin[u, row // (2 * QUARTER), row % (2 * QUARTER) : row % (2 * QUARTER) + 16, :] = jnp.concatenate(
-                [v, v], axis=1
-            )
+    for y_at in range(4):
+        for l_at in range(2):
+            first = y_at * 256 + l_at * 128
+            v = tok_ref[:, first : first + 128].astype(F32)
+            v = jnp.concatenate([v, v], axis=0).T.astype(BF16)
+            for group in range(8):
+                x_at, c_at = group // 2, group % 2
+                at = (2 * c_at + l_at) * 256 + y_at * 64 + x_at * 16
+                u, row = at // ROWS, at % ROWS
+                twin[u, row // (2 * QUARTER), row % (2 * QUARTER) : row % (2 * QUARTER) + 16, :] = (
+                    v[group * 16 : group * 16 + 16, :]
+                )
 
     pl.semaphore_wait(barrier, len(peers))
     first_swap = send(twin.at[:, 1 - c], twin_in, sibling)
@@ -318,25 +321,56 @@
         q = b // 2
         state["rest", q, p] = state.get(("rest", q, p), 0) + 1
         if state["rest", q, p] == 2:
-            state["low", q, p] = send(res.at[2 * q + (1 - l), p], pair_in.at[q, p], partner)
+            to_owner(q, p)
+
+    def to_owner(q, p):
+        n = len(sent)
+
+        def copy(src, slot, send_at, to):
+            return pltpu.make_async_remote_copy(
+                src_ref=src, dst_ref=ends.at[q, p, slot], send_sem=send_sem.at[send_at],
+                recv_sem=recv_sem.at[n + slot], device_id=to, device_id_type=MESH,
+            )
+
+        across = copy(res.at[2 * q + (1 - l), p], c, n, (k, gy(y, 1 - l, x, q)))
+        beside = copy(res.at[2 * q + l, p], 2, n + 1, sibling)
+        across.start()
+
+        @pl.when(c != q)
+        def _():
+            beside.start()
+
+        def sent_beside():
+            @pl.when(c != q)
+            def _():
+                beside.wait_send()
+
+        sent.extend((across.wait_send, sent_beside, lambda: None))
+        state["low", q, p] = [copy(res.at[2 * q + l, p], slot, n, sibling) for slot in range(3)]
 
     def low(i):
         q, p = i // 2, i % 2
-        state["low", q, p].wait_recv()
-        fin[q, p] = (res[2 * q + l, p] + pair_in[q, p]).astype(BF16)
-
-    def last(p):
-        state["last", p] = send(fin.at[1 - c, p], fin_in.at[p], sibling)
-        out_ref[:, pl.ds(pl.multiple_of(c * 2048 + p * 1024, 1024), 1024)] = fin[c, p]
-
-    steps = (pair, near, far, far_mid, far_end, up, z_on, act, h_on, down, mixed, mixed_end, rest_end, low, last)
-    for n, i in ORDER:
+
+        @pl.when(c == q)
+        def _():
+            for copy in state["low", q, p]:
+                copy.wait_recv()
+            own, other = res[2 * q + l, p] + ends[q, p, q], ends[q, p, 2] + ends[q, p, 1 - q]
+            out_ref[:, q * 2048 + p * 1024 : q * 2048 + p * 1024 + 1024] = own.astype(BF16)
+            at = (1 - q) * 2048 + p * 1024
+            out_ref[:, at : at + 1024] = other.astype(BF16)
+
+    steps = (pair, near, far, far_mid, far_end, up, z_on, act, h_on, down, mixed, mixed_end, rest_end, low)
+    settled = 0
+    for place, (n, i) in enumerate(ORDER):
+        if place >= len(ORDER) - 12:
+            until = min(settled + 40, len(sent) - 12)
+            for wait_send in sent[settled:until]:
+                wait_send()
+            settled = max(settled, until)
         steps[n](i)
-    for p in range(2):
-        state["last", p].wait_recv()
-        out_ref[:, pl.ds(pl.multiple_of((1 - c) * 2048 + p * 1024, 1024), 1024)] = fin_in[p]
-    for copy in sent:
-        copy.wait_send()
+    for wait_send in sent[settled:]:
+        wait_send()
     assert len(sent) <= MAX_SEMS
 
 
@@ -361,9 +395,7 @@
         pltpu.VMEM((2 * BLOCKS, 3, 16, 1024), REST),
         pltpu.VMEM((2 * BLOCKS, 3, 16, 1024), REST),
         pltpu.VMEM((BLOCKS, 2, 16, 1024), F32),
-        pltpu.VMEM((2, 2, 16, 1024), F32),
-        pltpu.VMEM((2, 2, 16, 1024), BF16),
-        pltpu.VMEM((2, 16, 1024), BF16),
+        pltpu.VMEM((2, 2, 3, 16, 1024), F32),
         pltpu.SemaphoreType.DMA((3,)),
         pltpu.SemaphoreType.DMA((MAX_SEMS,)),
         pltpu.SemaphoreType.DMA((MAX_SEMS,)),
@@ -379,7 +411,7 @@
         compiler_params=pltpu.CompilerParams(
             collective_id=0, has_side_effects=True, vmem_limit_bytes=62 * 2**20
         ),
-    )(tokens, gate_weight, up_weight, down_weight)
+    )(tokens.T, gate_weight, up_weight, down_weight)
 
 
 def solution(mesh):

time: 124 us -> 119 us (0.960)
  Pallas kernels: 120 us -> 118 us
  local copies, waits for them, and re-layouts: 3.3 us -> 1.57 us
    pallas_call x1, Pallas kernels: 120 us -> 118 us  [local(): pl.pallas_call(kernel, name='swiglu_layer', out_shape=jax.ShapeDtypeStruc...]
    unnamed x2 -> x1, local copies, waits for them, and re-layouts: 3.3 us -> 1.57 us
where the time goes in v3:
time: 119 us
  Pallas kernels  118 us (99%)
  local copies, waits for them, and re-layouts  1.57 us (1%)
    pallas_call x1, Pallas kernels, local(): pl.pallas_call(kernel, name='swiglu_layer', out_shape=jax.ShapeDtypeStruc...  118 us

profile of v3, /device:TPU:1, one launch (start us, length us, event | category | flops | bytes accessed | tf_op | source)
XLA Modules:
  0.0 119.3 jit_solution(11430137281627227807)
XLA Ops:
  0.0 117.7 %swiglu_layer.1 = bf16[16,4096]{1,0:T(8,128)(2,1)} custom-call(bf16[64,1024]{1,0:T(8,128)(2,1)} %bitcast.1, bf16[4096,512]{1,0:T(8,128)(2,1)} %wg_hbm.1, bf16[4096,512]{1,0:T(8,128)(2,1)} %wu_hbm.1, bf16[512,4096]{1,0:T(8,128)(2,1)} %wd_hbm.1), custom_call_target="tpu_custom_call" | custom-call | flops 12899999744 | bytes 13000000 | tf_op jit(solution)/shard_map/swiglu_layer/pallas_call | solution.py:403
  117.7 1.6 %copy.6 = bf16[16,4096]{1,0:T(8,128)(2,1)} copy(bf16[16,4096]{1,0:T(8,128)(2,1)} %swiglu_layer.1) | data formatting | bytes 262144

commit v4 on v3

--- a/solution.py
+++ b/solution.py
@@ -18,16 +18,15 @@
 MAX_SEMS = 384
 
 ORDER = (
-    (0, 0), (0, 4), (0, 3), (0, 1), (0, 7), (1, 0), (1, 3), (1, 1), (1, 4), (2, 0), (2, 1), (0, 6),
-    (2, 4), (0, 2), (1, 6), (3, 0), (4, 0), (2, 3), (1, 7), (1, 2), (3, 1), (4, 1), (5, 0), (5, 1),
-    (3, 4), (3, 3), (2, 6), (6, 0), (4, 3), (2, 2), (0, 5), (6, 1), (5, 3), (7, 0), (1, 5), (3, 6),
-    (7, 1), (3, 2), (4, 2), (4, 6), (6, 3), (4, 4), (2, 7), (5, 2), (5, 4), (3, 7), (2, 5), (6, 2),
-    (4, 7), (8, 1), (8, 0), (5, 6), (3, 5), (4, 5), (7, 2), (7, 3), (9, 1), (5, 5), (9, 0), (6, 4),
-    (8, 2), (10, 1), (8, 3), (6, 5), (5, 7), (10, 0), (7, 4), (9, 3), (9, 2), (7, 5), (6, 7), (10, 3),
-    (11, 1), (6, 6), (8, 4), (10, 2), (8, 5), (7, 7), (11, 0), (7, 6), (9, 5), (11, 3), (8, 7), (9, 4),
-    (8, 6), (10, 5), (10, 4), (9, 7), (9, 6), (10, 7), (10, 6), (11, 5), (11, 2), (11, 4), (12, 0), (12, 3),
-    (12, 1), (11, 7), (11, 6), (12, 2), (13, 0), (12, 5), (12, 4), (12, 7), (12, 6), (13, 3), (13, 1),
-    (13, 2),
+    (0, 6), (0, 2), (0, 7), (0, 3), (0, 1), (0, 0), (1, 6), (1, 2), (1, 3), (1, 1), (2, 6), (0, 4),
+    (2, 2), (1, 7), (2, 3), (1, 0), (3, 6), (4, 6), (2, 1), (3, 2), (5, 6), (4, 2), (0, 5), (1, 4),
+    (5, 2), (3, 3), (4, 3), (6, 6), (2, 7), (2, 0), (5, 3), (3, 7), (2, 4), (6, 2), (7, 6), (4, 7),
+    (6, 3), (5, 7), (3, 1), (7, 2), (1, 5), (4, 1), (5, 1), (2, 5), (3, 0), (4, 0), (7, 3), (6, 7),
+    (5, 0), (8, 3), (8, 2), (3, 5), (6, 1), (7, 7), (4, 5), (8, 6), (5, 5), (3, 4), (4, 4), (9, 3),
+    (9, 2), (8, 7), (6, 0), (5, 4), (10, 2), (7, 1), (10, 3), (9, 6), (7, 0), (9, 7), (6, 5), (10, 6),
+    (6, 4), (10, 7), (8, 1), (8, 0), (7, 5), (11, 3), (7, 4), (11, 2), (9, 1), (9, 0), (11, 6), (8, 4),
+    (11, 7), (8, 5), (10, 0), (10, 1), (9, 5), (9, 4), (12, 6), (10, 5), (10, 4), (11, 0), (12, 3), (11, 1),
+    (11, 4), (12, 7), (12, 2), (11, 5), (12, 0), (12, 1), (12, 4), (12, 5), (13, 2), (13, 1), (13, 0), (13, 3),
 )
 
 def kernel(

time: 119 us -> 117 us (0.983)
  Pallas kernels: 118 us -> 116 us
    pallas_call x1, Pallas kernels: 118 us -> 116 us  [local(): pl.pallas_call(kernel, name='swiglu_layer', out_shape=jax.ShapeDtypeStruc...]
where the time goes in v4:
time: 117 us
  Pallas kernels  116 us (99%)
  local copies, waits for them, and re-layouts  1.57 us (1%)
    pallas_call x1, Pallas kernels, local(): pl.pallas_call(kernel, name='swiglu_layer', out_shape=jax.ShapeDtypeStruc...  116 us

profile of v4, /device:TPU:1, one launch (start us, length us, event | category | flops | bytes accessed | tf_op | source)
XLA Modules:
  0.0 117.2 jit_solution(2291131363115013966)
XLA Ops:
  0.0 115.6 %swiglu_layer.1 = bf16[16,4096]{1,0:T(8,128)(2,1)} custom-call(bf16[64,1024]{1,0:T(8,128)(2,1)} %bitcast.1, bf16[4096,512]{1,0:T(8,128)(2,1)} %wg_hbm.1, bf16[4096,512]{1,0:T(8,128)(2,1)} %wu_hbm.1, bf16[512,4096]{1,0:T(8,128)(2,1)} %wd_hbm.1), custom_call_target="tpu_custom_call" | custom-call | flops 12899999744 | bytes 13000000 | tf_op jit(solution)/shard_map/swiglu_layer/pallas_call | solution.py:402
  115.6 1.6 %copy.6 = bf16[16,4096]{1,0:T(8,128)(2,1)} copy(bf16[16,4096]{1,0:T(8,128)(2,1)} %swiglu_layer.1) | data formatting | bytes 262144

commit v5 on v4

--- a/solution.py
+++ b/solution.py
@@ -55,18 +55,18 @@
     where = {"x": at_x, "y": at_y, "k": at_k}
     mine = {"x": x, "y": y, "k": k}
 
-    loads = []
-    for n, (src, dst) in enumerate(((wg_hbm, wg), (wu_hbm, wu), (wd_hbm, wd))):
-        copy = pltpu.make_async_copy(src, dst, load_sem.at[n])
-        copy.start()
-        loads.append(copy)
-
     barrier = pltpu.get_barrier_semaphore()
     peers = [sibling, partner, (k, gy(y, 1 - l, x, 1 - c))]
     peers += [at(d) for at in (at_x, at_y) for d in (1, 3, 2)]
     peers += [at_k(1), at_k(3)]
     for peer in peers:
         pl.semaphore_signal(barrier, inc=1, device_id=peer, device_id_type=MESH)
+
+    loads = []
+    for n, (src, dst) in enumerate(((wg_hbm, wg), (wu_hbm, wu), (wd_hbm, wd))):
+        copy = pltpu.make_async_copy(src, dst, load_sem.at[n])
+        copy.start()
+        loads.append(copy)
 
     sent = []
 
@@ -290,18 +290,18 @@
             got = jnp.dot(hid[b * PER : b * PER + PER].reshape(256, 512), wd[:, cols], preferred_element_type=F32)
             return got.reshape(4, 4, 16, 512)
 
-        @pl.loop(0, 2)
-        def _(n):
-            xs[i, :, :, :, pl.ds(pl.multiple_of(n * 512, 512), 512)] = tile(1 - c, n).astype(xs.dtype)
-
-        state["swap", i] = send(xs.at[i], xr.at[i], sibling)
+        state["swap", i] = []
+        for n in range(2):
+            at = (i, slice(None), slice(None), slice(None), slice(n * 512, n * 512 + 512))
+            xs[at] = tile(1 - c, n).astype(xs.dtype)
+            state["swap", i].append(send(xs.at[at], xr.at[at], sibling))
 
         @pl.loop(0, 2)
         def _(n):
             mix[i, :, :, :, pl.ds(pl.multiple_of(n * 512, 512), 512)] = tile(c, n)
 
     def mixed(i):
-        state["swap", i].wait_recv()
+        once(state["swap", i])
         if i % 2 == 0:
             read = lambda m: mix[i, m] + xr[i, m].astype(F32)
         else:
@@ -362,7 +362,7 @@
     steps = (pair, near, far, far_mid, far_end, up, z_on, act, h_on, down, mixed, mixed_end, rest_end, low)
     settled = 0
     for place, (n, i) in enumerate(ORDER):
-        if place >= len(ORDER) - 12:
+        if place >= len(ORDER) - 20:
             until = min(settled + 40, len(sent) - 12)
             for wait_send in sent[settled:until]:
                 wait_send()

time: 117 us -> 117 us (level)
  no operation moved by 1% of the time
where the time goes in v5:
time: 117 us
  Pallas kernels  115 us (98%)
  local copies, waits for them, and re-layouts  1.57 us (1%)
    pallas_call x1, Pallas kernels, local(): pl.pallas_call(kernel, name='swiglu_layer', out_shape=jax.ShapeDtypeStruc...  115 us

profile of v5, /device:TPU:1, one launch (start us, length us, event | category | flops | bytes accessed | tf_op | source)
XLA Modules:
  0.0 117.0 jit_solution(11161076199185954334)
XLA Ops:
  0.0 115.4 %swiglu_layer.1 = bf16[16,4096]{1,0:T(8,128)(2,1)} custom-call(bf16[64,1024]{1,0:T(8,128)(2,1)} %bitcast.1, bf16[4096,512]{1,0:T(8,128)(2,1)} %wg_hbm.1, bf16[4096,512]{1,0:T(8,128)(2,1)} %wu_hbm.1, bf16[512,4096]{1,0:T(8,128)(2,1)} %wd_hbm.1), custom_call_target="tpu_custom_call" | custom-call | flops 12899999744 | bytes 13000000 | tf_op jit(solution)/shard_map/swiglu_layer/pallas_call | solution.py:402
  115.4 1.6 %copy.6 = bf16[16,4096]{1,0:T(8,128)(2,1)} copy(bf16[16,4096]{1,0:T(8,128)(2,1)} %swiglu_layer.1) | data formatting | bytes 262144
